TPU v7x, 512 devices: a whole 4x4x16 slice. The times are simulated.
512 devices in a mesh: row: 32 (over y, x, core), col: 16 (over z).
Axes of the slice: x: 4, y: 4, z: 16, core: 2. Of those that a mesh axis runs over, the one named last changes fastest.
Arguments:
- tokens: bfloat16 [4096, 6144], P('row', 'col'), may hold values from -6 to 6
- weight_blocks: bfloat16 [16, 128, 4096], P('col', 'row'), may hold values from -0.375 to 0.375
- block_rows: int32 [16, 128], P('col', 'row'), may hold values from 0 to 95, as said below
- block_columns: int32 [16, 128], P('col', 'row'), may hold values from 0 to 47
- panel_counts: int32 [16], P('col'), may hold values from 16 to 128, as said below
- hidden_grad: bfloat16 [4096, 49152], P('row', 'col'), may hold values from -1.1953125 to 1.1953125
Outputs:
- hidden: bfloat16 [4096, 49152], P('row', 'col')
- input_grad: bfloat16 [4096, 6144], P('row', 'col')
- weight_grad: bfloat16 [16, 128, 4096], P('col', 'row')
Inputs may be any that keep to these rules, and one draw needn't show every extreme that they name: `block_rows`: in each panel the live slots name distinct pairs of block row and block column; ids in the other slots lie in the same ranges and mean nothing. `panel_counts`: some panel has all 128 slots live.
All inputs are finite; a program needn't handle non-finite values.
Results may differ from a plain program's by a relative error of at most 0.02.
Values may be sent and summed in bfloat16 or wider, within the bound.
No kernel may reach another device: no remote copies, remote signals or barrier semaphores. Data moves between devices by JAX's collectives and lax.ppermute only.
A program may use at most 64 MiB of HBM per device.

v0:
```python
import math
import jax
import jax.numpy as jnp
from jax import lax
from jax.sharding import PartitionSpec as P

root_two_pi = 0.7978845608028654
cubic_term = 0.044715


def gelu_value(pre_act):
    inner = root_two_pi * (pre_act + cubic_term * pre_act * pre_act * pre_act)
    return 0.5 * pre_act * (1.0 + jnp.tanh(inner))


def gelu_slope(pre_act):
    inner = root_two_pi * (pre_act + cubic_term * pre_act * pre_act * pre_act)
    tangent = jnp.tanh(inner)
    return 0.5 * (1.0 + tangent) + 0.5 * pre_act * (1.0 - tangent * tangent) * root_two_pi * (
        1.0 + 3.0 * cubic_term * pre_act * pre_act
    )


def grouped_inputs(blocks, rows_here, cols_here, live_here):
    length = rows_here.shape[0]
    stride = max([width for width in range(1, 65) if length % width == 0])
    group_count = length // stride
    block_side = math.isqrt(blocks.shape[-1])
    shaped = blocks.reshape(group_count, stride, block_side, block_side)
    return (
        shaped,
        rows_here.reshape(group_count, stride),
        cols_here.reshape(group_count, stride),
        live_here.reshape(group_count, stride),
    )


def forward_blocks(running_start, token_blocks, blocks, rows_here, cols_here, live_here):
    tok_rows = token_blocks.shape[0]
    block_side = token_blocks.shape[2]

    def forward_advance(running, inputs):
        part_blocks, part_rows, part_cols, part_live = inputs
        masked = jnp.where(part_live[:, None, None], part_blocks, jnp.zeros_like(part_blocks))
        picked = jnp.take(token_blocks, part_rows, axis=1)
        products = jnp.einsum("tsa,sab->stb", picked, masked, preferred_element_type=jnp.float32)
        return (
            running.at[part_cols].add(products.reshape(part_rows.shape[0], tok_rows * block_side)),
            None,
        )

    result, unused = lax.scan(
        forward_advance, running_start, grouped_inputs(blocks, rows_here, cols_here, live_here)
    )
    return result


def backward_blocks(running_start, grad_blocks, blocks, rows_here, cols_here, live_here):
    tok_rows = grad_blocks.shape[0]
    block_side = grad_blocks.shape[2]

    def backward_advance(running, inputs):
        part_blocks, part_rows, part_cols, part_live = inputs
        masked = jnp.where(part_live[:, None, None], part_blocks, jnp.zeros_like(part_blocks))
        picked = jnp.take(grad_blocks, part_cols, axis=1)
        products = jnp.einsum("tsb,sab->sta", picked, masked, preferred_element_type=jnp.float32)
        return (
            running.at[part_rows].add(products.reshape(part_rows.shape[0], tok_rows * block_side)),
            None,
        )

    result, unused = lax.scan(
        backward_advance, running_start, grouped_inputs(blocks, rows_here, cols_here, live_here)
    )
    return result


def on_device(tokens, weight_blocks, block_rows, block_columns, panel_counts, hidden_grad):
    whole = lax.all_gather(tokens, "col", axis=1, tiled=True)
    tok_rows = whole.shape[0]
    block_side = math.isqrt(weight_blocks.shape[2])
    row_blocks = whole.shape[1] // block_side
    col_blocks = hidden_grad.shape[1] // block_side
    per_device = weight_blocks.shape[1]
    capacity = per_device * lax.axis_size("row")
    count_live = panel_counts[0]
    token_blocks = whole.reshape(tok_rows, row_blocks, block_side)
    empty_pre = jnp.zeros((col_blocks, tok_rows * block_side), jnp.float32)
    empty_ids = jnp.zeros((capacity,), jnp.int32)
    shard_piece = (
        lax.all_gather(weight_blocks, "row", axis=1, tiled=True),
        lax.all_gather(block_rows, "row", axis=1, tiled=True),
        lax.all_gather(block_columns, "row", axis=1, tiled=True),
    )
    begin_at = jnp.int32(0)
    pre_sum = empty_pre
    fold_rows_all = empty_ids
    fold_cols_all = empty_ids
    rows_here = shard_piece[1][0]
    cols_here = shard_piece[2][0]
    live_here = jnp.arange(rows_here.shape[0], dtype=jnp.int32) < count_live
    pre_sum = forward_blocks(
        pre_sum, token_blocks, shard_piece[0][0], rows_here, cols_here, live_here
    )
    fold_rows_all = lax.dynamic_update_slice_in_dim(fold_rows_all, rows_here, begin_at, 0)
    fold_cols_all = lax.dynamic_update_slice_in_dim(fold_cols_all, cols_here, begin_at, 0)
    pre_sum, rows_all, cols_all = (pre_sum, fold_rows_all, fold_cols_all)
    pre_act = pre_sum.reshape(col_blocks, tok_rows, block_side).transpose(1, 0, 2)
    hidden = gelu_value(pre_act).astype(jnp.bfloat16).reshape(tok_rows, col_blocks * block_side)
    upstream = hidden_grad.reshape(tok_rows, col_blocks, block_side)
    grad_blocks = (upstream.astype(jnp.float32) * gelu_slope(pre_act)).astype(jnp.bfloat16)
    empty_back = jnp.zeros((row_blocks, tok_rows * block_side), jnp.float32)
    shard_piece = (
        lax.all_gather(weight_blocks, "row", axis=1, tiled=True),
        lax.all_gather(block_rows, "row", axis=1, tiled=True),
        lax.all_gather(block_columns, "row", axis=1, tiled=True),
    )
    rows_here = shard_piece[1][0]
    cols_here = shard_piece[2][0]
    live_here = jnp.arange(rows_here.shape[0], dtype=jnp.int32) < count_live
    input_part = backward_blocks(
        empty_back, grad_blocks, shard_piece[0][0], rows_here, cols_here, live_here
    )
    own_sums = lax.psum_scatter(
        input_part.astype(jnp.bfloat16), "col", scatter_dimension=0, tiled=True
    ).astype(jnp.float32)
    input_grad = (
        own_sums.reshape(-1, tok_rows, block_side)
        .transpose(1, 0, 2)
        .reshape(tok_rows, -1)
        .astype(jnp.bfloat16)
    )
    live_part = jnp.arange(per_device * lax.axis_size("row"), dtype=jnp.int32) < count_live
    picked_in = jnp.take(token_blocks, rows_all, axis=1)
    picked_grad = jnp.take(grad_blocks, cols_all, axis=1)
    products = jnp.einsum(
        "tsa,tsb->sab", picked_in, picked_grad, preferred_element_type=jnp.float32
    )
    products = jnp.where(live_part[:, None, None], products, jnp.zeros_like(products))
    weight_sum = lax.psum_scatter(
        products.reshape(per_device * lax.axis_size("row"), block_side * block_side).astype(
            jnp.bfloat16
        ),
        "row",
        scatter_dimension=0,
        tiled=True,
    )
    weight_grad = weight_sum.reshape(1, per_device, block_side * block_side)
    return (hidden, input_grad, weight_grad)


def solution(mesh):
    placed = (
        P("row", "col"),
        P("col", "row", None),
        P("col", "row"),
        P("col", "row"),
        P("col"),
        P("row", "col"),
    )
    return jax.shard_map(
        on_device,
        mesh=mesh,
        in_specs=placed,
        out_specs=(P("row", "col"), P("row", "col"), P("col", "row", None)),
        check_vma=False,
    )
```

profile of v0, /device:TPU:1, one launch (start us, length us, event | category | flops | bytes accessed | tf_op | source)
XLA Modules:
  0.0 446.8 jit_solution(2087213582369064578)
XLA Ops:
  15.8 14.4 %all-reduce.5 = (s32[128]{0:T(128)S(1)}, s32[128]{0:T(128)S(1)}) all-reduce(s32[128]{0:T(128)S(1)} %bitcast_dynamic-update-slice_fusion.1, s32[128]{0:T(128)S(1)} %bitcast_dynamic-update-slice_fusion), channel_id=1, replica_groups=mesh['row'=32,'col'=16] {'row'}, use_global_device_ids=true, to_apply=%add | all-reduce | flops 256 | bytes 2048 | tf_op jit(solution)/shard_map/squeeze | solution.py:100
  35.5 41.1 %all-gather.5.cloned.1.call-done = bf16[1,128,4096]{2,0,1:T(2,128)(2,1)} async-done(((bf16[1,4,4096]{2,0,1:T(2,128)(2,1)}), bf16[1,128,4096]{2,0,1:T(2,128)(2,1)}) %all-gather.5.cloned.1.call-update) | async-done | bytes 1048592 | tf_op jit(solution)/shard_map/all_gather | solution.py:91
  76.6 7.7 %reduce = bf16[128,4096]{1,0:T(8,128)(2,1)S(1)} reduce(bf16[1,128,4096]{2,0,1:T(2,128)(2,1)} %all-gather.5.cloned.1.call-done, bf16[]{:T(256)} %constant.132), dimensions={0}, to_apply=%all_gather.18.reduce_sub_computation | reduce | bytes 2097154 | tf_op jit(solution)/shard_map/all_gather | solution.py:91
  87.8 53.0 %all-gather.3.cloned.1.call-done = bf16[128,6144]{0,1:T(8,128)(2,1)} async-done(((bf16[128,384]{0,1:T(8,128)(2,1)}), bf16[128,6144]{0,1:T(8,128)(2,1)}) %all-gather.3.cloned.1.call-update) | async-done | bytes 1572880 | tf_op jit(solution)/shard_map/all_gather | solution.py:79
  140.9 40.8 %while.20 = (s32[]{:T(128)}, f32[48,8192]{1,0:T(8,128)S(1)}, s32[2,64]{1,0:T(2,128)S(1)}, s32[2,64]{1,0:T(2,128)S(1)}, bf16[128,96,64]{0,2,1:T(8,128)(2,1)}, /*i...) while((s32[]{:T(128)}, f32[48,8192]{1,0:T(8,128)S(1)}, s32[2,64]{1,0:T(2,128)S(1)}, ...), condition=%wide.region_2.3_spmd, body=%wide.region_0.2_spmd.sunk | while | flops 68421376 | bytes 18356652 | solution.py:52
  147.8 4.1 fusion.54
  151.9 4.8 %reshape.324 = f32[64,8192]{1,0:T(8,128)} reshape(f32[64,128,64]{2,1,0:T(8,128)} %fusion.54) | data formatting | bytes 4194304 | tf_op jit(solution)/shard_map/while/body/eval_jaxpr/reshape | solution.py:48
  156.7 4.6 %scatter_fusion = f32[48,8192]{1,0:T(8,128)S(1)} fusion(f32[48,8192]{1,0:T(8,128)S(1)} %get-tuple-element.269, s32[64]{0:T(128)S(1)} %get-tuple-element.249, f32[64,8192]{1,0:T(8,128)} %reshape.324), kind=kCustom, calls=%fused_computation.4.clone.1 | custom fusion | flops 524288 | bytes 6291712 | tf_op jit(solution)/shard_map/while/body/eval_jaxpr/scatter-add | solution.py:48
  168.1 4.1 fusion.54
  172.2 4.8 %reshape.324 = f32[64,8192]{1,0:T(8,128)} reshape(f32[64,128,64]{2,1,0:T(8,128)} %fusion.54) | data formatting | bytes 4194304 | tf_op jit(solution)/shard_map/while/body/eval_jaxpr/reshape | solution.py:48
  177.1 4.6 %scatter_fusion = f32[48,8192]{1,0:T(8,128)S(1)} fusion(f32[48,8192]{1,0:T(8,128)S(1)} %get-tuple-element.269, s32[64]{0:T(128)S(1)} %get-tuple-element.249, f32[64,8192]{1,0:T(8,128)} %reshape.324), kind=kCustom, calls=%fused_computation.4.clone.1 | custom fusion | flops 524288 | bytes 6291712 | tf_op jit(solution)/shard_map/while/body/eval_jaxpr/scatter-add | solution.py:48
  189.1 34.9 %while.21 = (s32[]{:T(128)}, f32[96,8192]{1,0:T(8,128)S(1)}, s32[2,64]{1,0:T(2,128)S(1)}, s32[2,64]{1,0:T(2,128)S(1)}, bf16[128,48,64]{0,2,1:T(8,128)(2,1)}, /*i...) while((s32[]{:T(128)}, f32[96,8192]{1,0:T(8,128)S(1)}, s32[2,64]{1,0:T(2,128)S(1)}, ...), condition=%wide.region_5.6_spmd, body=%wide.region_3.5_spmd.sunk | while | flops 68421376 | bytes 16783788 | solution.py:72
  192.2 4.4 fusion.57
  196.6 4.8 %reshape.329 = f32[64,8192]{1,0:T(8,128)} reshape(f32[64,128,64]{2,1,0:T(8,128)} %fusion.57) | data formatting | bytes 4194304 | tf_op jit(solution)/shard_map/while/body/eval_jaxpr/reshape | solution.py:68
  201.4 5.2 %scatter_fusion.1 = f32[96,8192]{1,0:T(8,128)S(1)} fusion(f32[96,8192]{1,0:T(8,128)S(1)} %get-tuple-element.293, s32[64]{0:T(128)S(1)} %get-tuple-element.258, f32[64,8192]{1,0:T(8,128)} %reshape.329), kind=kCustom, calls=%fused_computation.5.clone.1 | custom fusion | flops 524288 | bytes 6291712 | tf_op jit(solution)/shard_map/while/body/eval_jaxpr/scatter-add | solution.py:68
  209.5 4.4 fusion.57
  213.9 4.8 %reshape.329 = f32[64,8192]{1,0:T(8,128)} reshape(f32[64,128,64]{2,1,0:T(8,128)} %fusion.57) | data formatting | bytes 4194304 | tf_op jit(solution)/shard_map/while/body/eval_jaxpr/reshape | solution.py:68
  218.7 5.2 %scatter_fusion.1 = f32[96,8192]{1,0:T(8,128)S(1)} fusion(f32[96,8192]{1,0:T(8,128)S(1)} %get-tuple-element.293, s32[64]{0:T(128)S(1)} %get-tuple-element.258, f32[64,8192]{1,0:T(8,128)} %reshape.329), kind=kCustom, calls=%fused_computation.5.clone.1 | custom fusion | flops 524288 | bytes 6291712 | tf_op jit(solution)/shard_map/while/body/eval_jaxpr/scatter-add | solution.py:68
  225.3 33.0 %fusion = bf16[8,8192]{1,0:T(8,128)(2,1)S(1)} fusion(bf16[96,8192]{1,0:T(8,128)(2,1)} %convert_element_type.36), kind=kCustom, calls=%all-reduce-scatter | all-reduce-scatter fusion | flops 1048577 | bytes 1705984
  258.3 3.7 collective-permute-start.2
  261.9 4.3 collective-permute-start.1
  272.4 4.8 %fusion.27 = bf16[128,64,64]{2,1,0:T(8,128)(2,1)} fusion(bf16[128,128,64]{1,2,0:T(8,128)(2,1)} %gather_fusion.3, bf16[128,128,64]{1,2,0:T(8,128)(2,1)} %gather_fusion.2, pred[128]{0:T(512)(128)(4,1)S(1)} %copy-done.4, pred[128]{0:T(512)(128)(4,1)S(1)} %copy-done.5), kind=kOutput, calls=%fused_computation.53 | convolution fusion | flops 136314880 | bytes 5243136 | tf_op jit(solution)/shard_map/tsa,tsb->sab/dot_general | solution.py:136
  280.6 5.1 %collective-permute-start.3 = (bf16[6,8192]{1,0:T(8,128)(2,1)S(1)}, bf16[6,8192]{1,0:T(8,128)(2,1)S(1)}, u32[]{:S(2)}, u32[]{:S(2)}) collective-permute-start(bf16[6,8192]{1,0:T(8,128)(2,1)S(1)} %slice.8), channel_id=1, source_target_pairs={{0,4},{1,5},{2,6},{3,7},{4,8},{5,9},{6,10},{7,11},{8,12},{9,13},{1... | collective-permute-start | bytes 294920
  291.2 146.5 %all-reduce.8.cloned.1.call-done = bf16[128,4096]{0,1:T(8,128)(2,1)} async-done(((bf16[128,4096]{0,1:T(8,128)(2,1)}), bf16[128,4096]{0,1:T(8,128)(2,1)}) %all-reduce.8.cloned.1.call-update) | async-done | bytes 1048592
  (85 shorter events, 60.4 us)
Async XLA Ops:
  7.2 69.4 %all-gather.5.cloned.1.call-start = ((), (), s32[]{:S(2)}) async-start(), calls=%async_computation.1 | async-start | bytes 2162688 | tf_op jit(solution)/shard_map/all_gather | solution.py:91
  8.7 132.1 %all-gather.3.cloned.1.call-start = ((), (), s32[]{:S(2)}) async-start(), calls=%async_computation | async-start | bytes 1671168 | tf_op jit(solution)/shard_map/all_gather | solution.py:79
  10.4 427.3 %all-reduce.8.cloned.1.call-start = ((), (), s32[]{:S(2)}) async-start(), calls=%async_computation.2 | async-start | bytes 2097152
  225.3 42.3 %copy-start = (bf16[128,48,64]{0,2,1:T(8,128)(2,1)S(1)}, bf16[128,48,64]{0,2,1:T(8,128)(2,1)}, u32[]{:S(2)}) copy-start(bf16[128,48,64]{0,2,1:T(8,128)(2,1)} %get-tuple-element.311) | copy-start | bytes 2359300
  258.3 30.2 %collective-permute-start.2 = (bf16[8,8192]{1,0:T(8,128)(2,1)S(1)}, bf16[8,8192]{1,0:T(8,128)(2,1)S(1)}, u32[]{:S(2)}, u32[]{:S(2)}) collective-permute-start(bf16[8,8192]{1,0:T(8,128)(2,1)S(1)} %fusion), channel_id=1, source_target_pairs={{0,3},{1,4},{2,5},{3,6},{4,7},{5,8},{6,9},{7,10},{8,11},{9,12},{10... | collective-permute-start | bytes 393224
  261.9 26.6 %collective-permute-start.1 = (bf16[8,8192]{1,0:T(8,128)(2,1)S(1)}, bf16[8,8192]{1,0:T(8,128)(2,1)S(1)}, u32[]{:S(2)}, u32[]{:S(2)}) collective-permute-start(bf16[8,8192]{1,0:T(8,128)(2,1)S(1)} %fusion), channel_id=1, source_target_pairs={{0,2},{1,3},{2,4},{3,5},{4,6},{5,7},{6,8},{7,9},{8,10},{9,11},{10,... | collective-permute-start | bytes 393224
  266.2 22.2 %collective-permute-start = (bf16[8,8192]{1,0:T(8,128)(2,1)S(1)}, bf16[8,8192]{1,0:T(8,128)(2,1)S(1)}, u32[]{:S(2)}, u32[]{:S(2)}) collective-permute-start(bf16[8,8192]{1,0:T(8,128)(2,1)S(1)} %fusion), channel_id=1, source_target_pairs={{0,1},{1,2},{2,3},{3,4},{4,5},{5,6},{6,7},{7,8},{8,9},{9,10},{10,1... | collective-permute-start | bytes 393224
  267.5 2.4 copy-start.1
  270.0 2.4 copy-start.4
  270.0 2.4 copy-start.5
  277.2 8.5 %copy-start.3 = (pred[128]{0:T(512)(128)(4,1)S(1)}, pred[128]{0:T(512)(128)(4,1)}, u32[]{:S(2)}) copy-start(pred[128]{0:T(512)(128)(4,1)} %iota_compare_fusion) | copy-start | bytes 388
  277.2 9.8 %copy-start.2 = (bf16[128,48,64]{0,2,1:T(8,128)(2,1)S(1)}, bf16[128,48,64]{0,2,1:T(8,128)(2,1)}, u32[]{:S(2)}) copy-start(bf16[128,48,64]{0,2,1:T(8,128)(2,1)} %get-tuple-element.161) | copy-start | bytes 2359300
  280.6 7.9 %collective-permute-start.3 = (bf16[6,8192]{1,0:T(8,128)(2,1)S(1)}, bf16[6,8192]{1,0:T(8,128)(2,1)S(1)}, u32[]{:S(2)}, u32[]{:S(2)}) collective-permute-start(bf16[6,8192]{1,0:T(8,128)(2,1)S(1)} %slice.8), channel_id=1, source_target_pairs={{0,4},{1,5},{2,6},{3,7},{4,8},{5,9},{6,10},{7,11},{8,12},{9,13},{1... | collective-permute-start | bytes 294920
Sparse Core Ops, SparseCore 0:
  11.7 64.8 all-gather.4
  79.3 61.5 all-gather.2
  288.3 149.3 all-reduce.7
where the time goes:
time: 448 us; the launch traced here: 447 us
  waiting for transfers between devices  241 us (54%)
  local copies, waits for them, and re-layouts  70.5 us (16%)
  blocking collectives  47.4 us (11%)
  other arithmetic  34.7 us (8%)
  matrix products  21.9 us (5%)
  between operations  16.4 us (4%)
  starting transfers between devices  14.4 us (3%)
    unnamed x8, waiting for transfers between devices  147 us
    all_gather x1, waiting for transfers between devices, on_device(): whole = lax.all_gather(tokens, 'col', axis=1, tiled=True)  53 us
    all_gather x1, waiting for transfers between devices, on_device(): lax.all_gather(weight_blocks, 'row', axis=1, tiled=True)  41.1 us
    unnamed x1, blocking collectives  33 us
    squeeze x1, blocking collectives, on_device(): cols_here = shard_piece[2][0]  14.4 us
    unnamed x5, starting transfers between devices  14.4 us
    unnamed x27, local copies, waits for them, and re-layouts  13.3 us
    scatter-add x2, other arithmetic, backward_advance(): running.at[part_rows]  10.4 us
  transfers between devices with their start and end apart: 7, of which 4 were waited for; matrix products, arithmetic and copies ran while one was open for 9% of the time, Pallas kernels for 0%

commit v1 on v0

--- a/solution.py
+++ b/solution.py
@@ -76,7 +76,34 @@
 
 
 def on_device(tokens, weight_blocks, block_rows, block_columns, panel_counts, hidden_grad):
-    whole = lax.all_gather(tokens, "col", axis=1, tiled=True)
+
+    def raise_pipes_in(content, chip_axis="col"):
+        piece_out = jax.lax.axis_size(chip_axis)
+        found_now = jax.lax.axis_index(chip_axis)
+        w_next, q_next, low = (piece_out, found_now, content.shape[1])
+        small = range(w_next)
+        r_now = map(lambda dd: (dd, (dd + 1) % w_next), small)
+        gallery = list(r_now)
+        parts_out = range(w_next)
+        r2 = map(lambda dd: (dd, (dd - 1) % w_next), parts_out)
+        series = list(r2)
+        n_now = jnp.zeros((*content.shape[:1], w_next * low, *content.shape[2:]), content.dtype)
+        n_now = lax.dynamic_update_slice_in_dim(n_now, content, q_next * low, axis=1)
+        carry_in = upper = content
+        latest = w_next // 2
+        for j0 in tuple(range(1, latest + 1)):
+            carry_in = jax.lax.ppermute(carry_in, axis_name=chip_axis, perm=gallery)
+            n_now = lax.dynamic_update_slice_in_dim(
+                n_now, carry_in, (q_next - j0) % w_next * low, axis=1
+            )
+            if j0 < w_next - latest:
+                upper = jax.lax.ppermute(upper, axis_name=chip_axis, perm=series)
+                n_now = lax.dynamic_update_slice_in_dim(
+                    n_now, upper, (q_next + j0) % w_next * low, axis=1
+                )
+        return n_now
+
+    whole = raise_pipes_in(tokens)
     tok_rows = whole.shape[0]
     block_side = math.isqrt(weight_blocks.shape[2])
     row_blocks = whole.shape[1] // block_side

time: 448 us -> 417 us (0.931)
  waiting for transfers between devices: 241 us -> 155 us
  starting transfers between devices: 14.4 us -> 69.6 us
    ppermute x0 -> x15, starting transfers between devices: none -> 56.3 us  [the longest x7 41 us: raise_pipes_in(): upper = jax.lax.ppermute(upper, axis_name=chip_axis, perm=series)]
    all_gather x1 -> x0, waiting for transfers between devices: 53 us -> none  [on_device(): whole = lax.all_gather(tokens, 'col', axis=1, tiled=True)]
    all_gather x1, waiting for transfers between devices: 41.1 us -> 0.01 us  [on_device(): lax.all_gather(weight_blocks, 'row', axis=1, tiled=True)]
    ppermute x0 -> x15, waiting for transfers between devices: none -> 9.78 us  [the longest x8 9.55 us: raise_pipes_in(): carry_in = jax.lax.ppermute(carry_in, axis_name=chip_axis, perm=gallery)]
    unnamed x8 -> x7, waiting for transfers between devices: 147 us -> 145 us
    unnamed x27 -> x29, local copies, waits for them, and re-layouts: 13.3 us -> 12.8 us
  transfers between devices with their start and end apart: 7 -> 21, of which waited for: 4 -> 5; matrix products, arithmetic and copies ran while one was open for 9% -> 6% of each run, Pallas kernels for 0% -> 0%
where the time goes in v1:
time: 417 us; the launch traced here: 415 us
  waiting for transfers between devices  155 us (37%)
  local copies, waits for them, and re-layouts  70.3 us (17%)
  starting transfers between devices  69.6 us (17%)
  blocking collectives  47.6 us (11%)
  other arithmetic  34.1 us (8%)
  matrix products  21.2 us (5%)
  between operations  17.5 us (4%)
    unnamed x7, waiting for transfers between devices  145 us
    ppermute x7, starting transfers between devices, raise_pipes_in(): upper = jax.lax.ppermute(upper, axis_name=chip_axis, perm=series)  41 us
    unnamed x1, blocking collectives  33.7 us
    ppermute x8, starting transfers between devices, raise_pipes_in(): carry_in = jax.lax.ppermute(carry_in, axis_name=chip_axis, perm=gallery)  15.3 us
    squeeze x1, blocking collectives, on_device(): cols_here = shard_piece[2][0]  13.9 us
    unnamed x5, starting transfers between devices  13.2 us
    unnamed x29, local copies, waits for them, and re-layouts  12.8 us
    scatter-add x2, other arithmetic, backward_advance(): running.at[part_rows]  10.4 us
  transfers between devices with their start and end apart: 21, of which 5 were waited for; matrix products, arithmetic and copies ran while one was open for 6% of the time, Pallas kernels for 0%

profile of v1, /device:TPU:1, one launch (start us, length us, event | category | flops | bytes accessed | tf_op | source)
XLA Modules:
  0.0 415.3 jit_solution(16231112744114037665)
XLA Ops:
  8.2 12.0 %collective-permute-start.1 = (bf16[128,384]{0,1:T(8,128)(2,1)S(1)}, bf16[128,384]{0,1:T(8,128)(2,1)S(1)}, u32[]{:S(2)}, u32[]{:S(2)}) collective-permute-start(bf16[128,384]{0,1:T(8,128)(2,1)S(1)} %copy.58), channel_id=1, source_target_pairs={{0,15},{1,0},{2,1},{3,2},{4,3},{5,4},{6,5},{7,6},{8,7},{9,8},{10,9... | collective-permute-start | bytes 294920 | tf_op jit(solution)/shard_map/ppermute | solution.py:100
  27.2 13.9 %all-reduce.5 = (s32[128]{0:T(128)S(1)}, s32[128]{0:T(128)S(1)}) all-reduce(s32[128]{0:T(128)S(1)} %bitcast_dynamic-update-slice_fusion.1, s32[128]{0:T(128)S(1)} %bitcast_dynamic-update-slice_fusion), channel_id=1, replica_groups=mesh['row'=32,'col'=16] {'row'}, use_global_device_ids=true, to_apply=%add | all-reduce | flops 256 | bytes 2048 | tf_op jit(solution)/shard_map/squeeze | solution.py:127
  48.3 4.8 %collective-permute-start.3 = (bf16[128,384]{0,1:T(8,128)(2,1)S(1)}, bf16[128,384]{0,1:T(8,128)(2,1)S(1)}, u32[]{:S(2)}, u32[]{:S(2)}) collective-permute-start(bf16[128,384]{0,1:T(8,128)(2,1)S(1)} %collective-permute-done.1), channel_id=1, source_target_pairs={{0,15},{1,0},{2,1},{3,2},{4,3},{5,4},{6,5},{7,6},{8,7},{9,8},{10,9... | collective-permute-start | bytes 294920 | tf_op jit(solution)/shard_map/ppermute | solution.py:100
  55.1 4.6 %collective-permute-start.5 = (bf16[128,384]{0,1:T(8,128)(2,1)S(1)}, bf16[128,384]{0,1:T(8,128)(2,1)S(1)}, u32[]{:S(2)}, u32[]{:S(2)}) collective-permute-start(bf16[128,384]{0,1:T(8,128)(2,1)S(1)} %collective-permute-done.3), channel_id=1, source_target_pairs={{0,15},{1,0},{2,1},{3,2},{4,3},{5,4},{6,5},{7,6},{8,7},{9,8},{10,9... | collective-permute-start | bytes 294920 | tf_op jit(solution)/shard_map/ppermute | solution.py:100
  61.7 4.6 %collective-permute-start.7 = (bf16[128,384]{0,1:T(8,128)(2,1)S(1)}, bf16[128,384]{0,1:T(8,128)(2,1)S(1)}, u32[]{:S(2)}, u32[]{:S(2)}) collective-permute-start(bf16[128,384]{0,1:T(8,128)(2,1)S(1)} %collective-permute-done.5), channel_id=1, source_target_pairs={{0,15},{1,0},{2,1},{3,2},{4,3},{5,4},{6,5},{7,6},{8,7},{9,8},{10,9... | collective-permute-start | bytes 294920 | tf_op jit(solution)/shard_map/ppermute | solution.py:100
  68.3 4.6 %collective-permute-start.9 = (bf16[128,384]{0,1:T(8,128)(2,1)S(1)}, bf16[128,384]{0,1:T(8,128)(2,1)S(1)}, u32[]{:S(2)}, u32[]{:S(2)}) collective-permute-start(bf16[128,384]{0,1:T(8,128)(2,1)S(1)} %collective-permute-done.7), channel_id=1, source_target_pairs={{0,15},{1,0},{2,1},{3,2},{4,3},{5,4},{6,5},{7,6},{8,7},{9,8},{10,9... | collective-permute-start | bytes 294920 | tf_op jit(solution)/shard_map/ppermute | solution.py:100
  75.4 5.4 %collective-permute-start.11 = (bf16[128,384]{0,1:T(8,128)(2,1)S(1)}, bf16[128,384]{0,1:T(8,128)(2,1)S(1)}, u32[]{:S(2)}, u32[]{:S(2)}) collective-permute-start(bf16[128,384]{0,1:T(8,128)(2,1)S(1)} %collective-permute-done.9), channel_id=1, source_target_pairs={{0,15},{1,0},{2,1},{3,2},{4,3},{5,4},{6,5},{7,6},{8,7},{9,8},{10,9... | collective-permute-start | bytes 294920 | tf_op jit(solution)/shard_map/ppermute | solution.py:100
  82.8 5.1 %collective-permute-start.13 = (bf16[128,384]{0,1:T(8,128)(2,1)S(1)}, bf16[128,384]{0,1:T(8,128)(2,1)S(1)}, u32[]{:S(2)}, u32[]{:S(2)}) collective-permute-start(bf16[128,384]{0,1:T(8,128)(2,1)S(1)} %collective-permute-done.11), channel_id=1, source_target_pairs={{0,15},{1,0},{2,1},{3,2},{4,3},{5,4},{6,5},{7,6},{8,7},{9,8},{10,9... | collective-permute-start | bytes 294920 | tf_op jit(solution)/shard_map/ppermute | solution.py:100
  89.9 4.6 %collective-permute-done.12 = bf16[128,384]{0,1:T(8,128)(2,1)S(1)} collective-permute-done((bf16[128,384]{0,1:T(8,128)(2,1)S(1)}, bf16[128,384]{0,1:T(8,128)(2,1)S(1)}, u32[]{:S(2)}, u32[]{:S(2)}) %collective-permute-start.12) | collective-permute-done | bytes 98336 | tf_op jit(solution)/shard_map/ppermute | solution.py:95
  96.5 4.6 %collective-permute-done.14 = bf16[128,384]{0,1:T(8,128)(2,1)S(1)} collective-permute-done((bf16[128,384]{0,1:T(8,128)(2,1)S(1)}, bf16[128,384]{0,1:T(8,128)(2,1)S(1)}, u32[]{:S(2)}, u32[]{:S(2)}) %collective-permute-start.14) | collective-permute-done | bytes 98336 | tf_op jit(solution)/shard_map/ppermute | solution.py:95
  103.3 7.7 %reduce = bf16[128,4096]{1,0:T(8,128)(2,1)S(1)} reduce(bf16[1,128,4096]{2,0,1:T(2,128)(2,1)} %all-gather.2.cloned.1.call-done, bf16[]{:T(256)} %constant.241), dimensions={0}, to_apply=%all_gather.14.reduce_sub_computation | reduce | bytes 2097154 | tf_op jit(solution)/shard_map/all_gather | solution.py:118
  114.6 40.8 %while.20 = (s32[]{:T(128)}, f32[48,8192]{1,0:T(8,128)S(1)}, s32[2,64]{1,0:T(2,128)S(1)}, s32[2,64]{1,0:T(2,128)S(1)}, bf16[128,96,64]{0,2,1:T(8,128)(2,1)}, /*i...) while((s32[]{:T(128)}, f32[48,8192]{1,0:T(8,128)S(1)}, s32[2,64]{1,0:T(2,128)S(1)}, ...), condition=%wide.region_2.3_spmd, body=%wide.region_0.2_spmd.sunk | while | flops 68421376 | bytes 18356652 | solution.py:52
  125.6 4.8 %reshape.324 = f32[64,8192]{1,0:T(8,128)} reshape(f32[64,128,64]{2,1,0:T(8,128)} %fusion.54) | data formatting | bytes 4194304 | tf_op jit(solution)/shard_map/while/body/eval_jaxpr/reshape | solution.py:48
  130.4 4.6 %scatter_fusion = f32[48,8192]{1,0:T(8,128)S(1)} fusion(f32[48,8192]{1,0:T(8,128)S(1)} %get-tuple-element.269, s32[64]{0:T(128)S(1)} %get-tuple-element.249, f32[64,8192]{1,0:T(8,128)} %reshape.324), kind=kCustom, calls=%fused_computation.4.clone.1 | custom fusion | flops 524288 | bytes 6291712 | tf_op jit(solution)/shard_map/while/body/eval_jaxpr/scatter-add | solution.py:48
  146.0 4.8 %reshape.324 = f32[64,8192]{1,0:T(8,128)} reshape(f32[64,128,64]{2,1,0:T(8,128)} %fusion.54) | data formatting | bytes 4194304 | tf_op jit(solution)/shard_map/while/body/eval_jaxpr/reshape | solution.py:48
  150.8 4.6 %scatter_fusion = f32[48,8192]{1,0:T(8,128)S(1)} fusion(f32[48,8192]{1,0:T(8,128)S(1)} %get-tuple-element.269, s32[64]{0:T(128)S(1)} %get-tuple-element.249, f32[64,8192]{1,0:T(8,128)} %reshape.324), kind=kCustom, calls=%fused_computation.4.clone.1 | custom fusion | flops 524288 | bytes 6291712 | tf_op jit(solution)/shard_map/while/body/eval_jaxpr/scatter-add | solution.py:48
  162.8 35.0 %while.21 = (s32[]{:T(128)}, f32[96,8192]{1,0:T(8,128)S(1)}, s32[2,64]{1,0:T(2,128)S(1)}, s32[2,64]{1,0:T(2,128)S(1)}, bf16[128,48,64]{0,2,1:T(8,128)(2,1)}, /*i...) while((s32[]{:T(128)}, f32[96,8192]{1,0:T(8,128)S(1)}, s32[2,64]{1,0:T(2,128)S(1)}, ...), condition=%wide.region_5.6_spmd, body=%wide.region_3.5_spmd.sunk | while | flops 68421376 | bytes 16783788 | solution.py:72
  170.4 4.8 %reshape.329 = f32[64,8192]{1,0:T(8,128)} reshape(f32[64,128,64]{2,1,0:T(8,128)} %fusion.57) | data formatting | bytes 4194304 | tf_op jit(solution)/shard_map/while/body/eval_jaxpr/reshape | solution.py:68
  175.2 5.2 %scatter_fusion.1 = f32[96,8192]{1,0:T(8,128)S(1)} fusion(f32[96,8192]{1,0:T(8,128)S(1)} %get-tuple-element.293, s32[64]{0:T(128)S(1)} %get-tuple-element.258, f32[64,8192]{1,0:T(8,128)} %reshape.329), kind=kCustom, calls=%fused_computation.5.clone.1 | custom fusion | flops 524288 | bytes 6291712 | tf_op jit(solution)/shard_map/while/body/eval_jaxpr/scatter-add | solution.py:68
  187.7 4.8 %reshape.329 = f32[64,8192]{1,0:T(8,128)} reshape(f32[64,128,64]{2,1,0:T(8,128)} %fusion.57) | data formatting | bytes 4194304 | tf_op jit(solution)/shard_map/while/body/eval_jaxpr/reshape | solution.py:68
  192.5 5.2 %scatter_fusion.1 = f32[96,8192]{1,0:T(8,128)S(1)} fusion(f32[96,8192]{1,0:T(8,128)S(1)} %get-tuple-element.293, s32[64]{0:T(128)S(1)} %get-tuple-element.258, f32[64,8192]{1,0:T(8,128)} %reshape.329), kind=kCustom, calls=%fused_computation.5.clone.1 | custom fusion | flops 524288 | bytes 6291712 | tf_op jit(solution)/shard_map/while/body/eval_jaxpr/scatter-add | solution.py:68
  199.1 33.7 %fusion = bf16[8,8192]{1,0:T(8,128)(2,1)S(1)} fusion(bf16[96,8192]{1,0:T(8,128)(2,1)} %convert_element_type.36), kind=kCustom, calls=%all-reduce-scatter | all-reduce-scatter fusion | flops 1048577 | bytes 1705984
  249.1 6.8 %collective-permute-start.18 = (bf16[6,8192]{1,0:T(8,128)(2,1)S(1)}, bf16[6,8192]{1,0:T(8,128)(2,1)S(1)}, u32[]{:S(2)}, u32[]{:S(2)}) collective-permute-start(bf16[6,8192]{1,0:T(8,128)(2,1)S(1)} %slice.8), channel_id=1, source_target_pairs={{0,4},{1,5},{2,6},{3,7},{4,8},{5,9},{6,10},{7,11},{8,12},{9,13},{1... | collective-permute-start | bytes 294920
  261.1 144.8 %all-reduce.8.cloned.1.call-done = bf16[128,4096]{0,1:T(8,128)(2,1)} async-done(((bf16[128,4096]{0,1:T(8,128)(2,1)}), bf16[128,4096]{0,1:T(8,128)(2,1)}) %all-reduce.8.cloned.1.call-update) | async-done | bytes 1048592
  (131 shorter events, 101.5 us)
Async XLA Ops:
  7.2 96.1 %all-gather.2.cloned.1.call-start = ((), (), s32[]{:S(2)}) async-start(), calls=%async_computation | async-start | bytes 2162688 | tf_op jit(solution)/shard_map/all_gather | solution.py:118
  8.2 40.0 %collective-permute-start.1 = (bf16[128,384]{0,1:T(8,128)(2,1)S(1)}, bf16[128,384]{0,1:T(8,128)(2,1)S(1)}, u32[]{:S(2)}, u32[]{:S(2)}) collective-permute-start(bf16[128,384]{0,1:T(8,128)(2,1)S(1)} %copy.58), channel_id=1, source_target_pairs={{0,15},{1,0},{2,1},{3,2},{4,3},{5,4},{6,5},{7,6},{8,7},{9,8},{10,9... | collective-permute-start | bytes 294920 | tf_op jit(solution)/shard_map/ppermute | solution.py:100
  20.2 32.9 %collective-permute-start = (bf16[128,384]{0,1:T(8,128)(2,1)S(1)}, bf16[128,384]{0,1:T(8,128)(2,1)S(1)}, u32[]{:S(2)}, u32[]{:S(2)}) collective-permute-start(bf16[128,384]{0,1:T(8,128)(2,1)S(1)} %copy.58), channel_id=1, source_target_pairs={{0,1},{1,2},{2,3},{3,4},{4,5},{5,6},{6,7},{7,8},{8,9},{9,10},{10,1... | collective-permute-start | bytes 294920 | tf_op jit(solution)/shard_map/ppermute | solution.py:95
  23.6 382.3 %all-reduce.8.cloned.1.call-start = ((), (), s32[]{:S(2)}) async-start(), calls=%async_computation.1 | async-start | bytes 2097152
  48.3 6.8 %collective-permute-start.3 = (bf16[128,384]{0,1:T(8,128)(2,1)S(1)}, bf16[128,384]{0,1:T(8,128)(2,1)S(1)}, u32[]{:S(2)}, u32[]{:S(2)}) collective-permute-start(bf16[128,384]{0,1:T(8,128)(2,1)S(1)} %collective-permute-done.1), channel_id=1, source_target_pairs={{0,15},{1,0},{2,1},{3,2},{4,3},{5,4},{6,5},{7,6},{8,7},{9,8},{10,9... | collective-permute-start | bytes 294920 | tf_op jit(solution)/shard_map/ppermute | solution.py:100
  53.1 6.6 %collective-permute-start.2 = (bf16[128,384]{0,1:T(8,128)(2,1)S(1)}, bf16[128,384]{0,1:T(8,128)(2,1)S(1)}, u32[]{:S(2)}, u32[]{:S(2)}) collective-permute-start(bf16[128,384]{0,1:T(8,128)(2,1)S(1)} %collective-permute-done), channel_id=1, source_target_pairs={{0,1},{1,2},{2,3},{3,4},{4,5},{5,6},{6,7},{7,8},{8,9},{9,10},{10,1... | collective-permute-start | bytes 294920 | tf_op jit(solution)/shard_map/ppermute | solution.py:95
  55.1 6.6 %collective-permute-start.5 = (bf16[128,384]{0,1:T(8,128)(2,1)S(1)}, bf16[128,384]{0,1:T(8,128)(2,1)S(1)}, u32[]{:S(2)}, u32[]{:S(2)}) collective-permute-start(bf16[128,384]{0,1:T(8,128)(2,1)S(1)} %collective-permute-done.3), channel_id=1, source_target_pairs={{0,15},{1,0},{2,1},{3,2},{4,3},{5,4},{6,5},{7,6},{8,7},{9,8},{10,9... | collective-permute-start | bytes 294920 | tf_op jit(solution)/shard_map/ppermute | solution.py:100
  59.7 6.6 %collective-permute-start.4 = (bf16[128,384]{0,1:T(8,128)(2,1)S(1)}, bf16[128,384]{0,1:T(8,128)(2,1)S(1)}, u32[]{:S(2)}, u32[]{:S(2)}) collective-permute-start(bf16[128,384]{0,1:T(8,128)(2,1)S(1)} %collective-permute-done.2), channel_id=1, source_target_pairs={{0,1},{1,2},{2,3},{3,4},{4,5},{5,6},{6,7},{7,8},{8,9},{9,10},{10,1... | collective-permute-start | bytes 294920 | tf_op jit(solution)/shard_map/ppermute | solution.py:95
  61.7 6.6 %collective-permute-start.7 = (bf16[128,384]{0,1:T(8,128)(2,1)S(1)}, bf16[128,384]{0,1:T(8,128)(2,1)S(1)}, u32[]{:S(2)}, u32[]{:S(2)}) collective-permute-start(bf16[128,384]{0,1:T(8,128)(2,1)S(1)} %collective-permute-done.5), channel_id=1, source_target_pairs={{0,15},{1,0},{2,1},{3,2},{4,3},{5,4},{6,5},{7,6},{8,7},{9,8},{10,9... | collective-permute-start | bytes 294920 | tf_op jit(solution)/shard_map/ppermute | solution.py:100
  66.3 6.9 %collective-permute-start.6 = (bf16[128,384]{0,1:T(8,128)(2,1)S(1)}, bf16[128,384]{0,1:T(8,128)(2,1)S(1)}, u32[]{:S(2)}, u32[]{:S(2)}) collective-permute-start(bf16[128,384]{0,1:T(8,128)(2,1)S(1)} %collective-permute-done.4), channel_id=1, source_target_pairs={{0,1},{1,2},{2,3},{3,4},{4,5},{5,6},{6,7},{7,8},{8,9},{9,10},{10,1... | collective-permute-start | bytes 294920 | tf_op jit(solution)/shard_map/ppermute | solution.py:95
  68.3 7.1 %collective-permute-start.9 = (bf16[128,384]{0,1:T(8,128)(2,1)S(1)}, bf16[128,384]{0,1:T(8,128)(2,1)S(1)}, u32[]{:S(2)}, u32[]{:S(2)}) collective-permute-start(bf16[128,384]{0,1:T(8,128)(2,1)S(1)} %collective-permute-done.7), channel_id=1, source_target_pairs={{0,15},{1,0},{2,1},{3,2},{4,3},{5,4},{6,5},{7,6},{8,7},{9,8},{10,9... | collective-permute-start | bytes 294920 | tf_op jit(solution)/shard_map/ppermute | solution.py:100
  73.2 7.6 %collective-permute-start.8 = (bf16[128,384]{0,1:T(8,128)(2,1)S(1)}, bf16[128,384]{0,1:T(8,128)(2,1)S(1)}, u32[]{:S(2)}, u32[]{:S(2)}) collective-permute-start(bf16[128,384]{0,1:T(8,128)(2,1)S(1)} %collective-permute-done.6), channel_id=1, source_target_pairs={{0,1},{1,2},{2,3},{3,4},{4,5},{5,6},{6,7},{7,8},{8,9},{9,10},{10,1... | collective-permute-start | bytes 294920 | tf_op jit(solution)/shard_map/ppermute | solution.py:95
  75.4 7.4 %collective-permute-start.11 = (bf16[128,384]{0,1:T(8,128)(2,1)S(1)}, bf16[128,384]{0,1:T(8,128)(2,1)S(1)}, u32[]{:S(2)}, u32[]{:S(2)}) collective-permute-start(bf16[128,384]{0,1:T(8,128)(2,1)S(1)} %collective-permute-done.9), channel_id=1, source_target_pairs={{0,15},{1,0},{2,1},{3,2},{4,3},{5,4},{6,5},{7,6},{8,7},{9,8},{10,9... | collective-permute-start | bytes 294920 | tf_op jit(solution)/shard_map/ppermute | solution.py:100
  80.9 7.1 %collective-permute-start.10 = (bf16[128,384]{0,1:T(8,128)(2,1)S(1)}, bf16[128,384]{0,1:T(8,128)(2,1)S(1)}, u32[]{:S(2)}, u32[]{:S(2)}) collective-permute-start(bf16[128,384]{0,1:T(8,128)(2,1)S(1)} %collective-permute-done.8), channel_id=1, source_target_pairs={{0,1},{1,2},{2,3},{3,4},{4,5},{5,6},{6,7},{7,8},{8,9},{9,10},{10,1... | collective-permute-start | bytes 294920 | tf_op jit(solution)/shard_map/ppermute | solution.py:95
  82.8 13.6 %collective-permute-start.13 = (bf16[128,384]{0,1:T(8,128)(2,1)S(1)}, bf16[128,384]{0,1:T(8,128)(2,1)S(1)}, u32[]{:S(2)}, u32[]{:S(2)}) collective-permute-start(bf16[128,384]{0,1:T(8,128)(2,1)S(1)} %collective-permute-done.11), channel_id=1, source_target_pairs={{0,15},{1,0},{2,1},{3,2},{4,3},{5,4},{6,5},{7,6},{8,7},{9,8},{10,9... | collective-permute-start | bytes 294920 | tf_op jit(solution)/shard_map/ppermute | solution.py:100
  87.9 6.6 %collective-permute-start.12 = (bf16[128,384]{0,1:T(8,128)(2,1)S(1)}, bf16[128,384]{0,1:T(8,128)(2,1)S(1)}, u32[]{:S(2)}, u32[]{:S(2)}) collective-permute-start(bf16[128,384]{0,1:T(8,128)(2,1)S(1)} %collective-permute-done.10), channel_id=1, source_target_pairs={{0,1},{1,2},{2,3},{3,4},{4,5},{5,6},{6,7},{7,8},{8,9},{9,10},{10,1... | collective-permute-start | bytes 294920 | tf_op jit(solution)/shard_map/ppermute | solution.py:95
  94.5 6.6 %collective-permute-start.14 = (bf16[128,384]{0,1:T(8,128)(2,1)S(1)}, bf16[128,384]{0,1:T(8,128)(2,1)S(1)}, u32[]{:S(2)}, u32[]{:S(2)}) collective-permute-start(bf16[128,384]{0,1:T(8,128)(2,1)S(1)} %collective-permute-done.12), channel_id=1, source_target_pairs={{0,1},{1,2},{2,3},{3,4},{4,5},{5,6},{6,7},{7,8},{8,9},{9,10},{10,1... | collective-permute-start | bytes 294920 | tf_op jit(solution)/shard_map/ppermute | solution.py:95
  199.1 40.2 %copy-start = (bf16[128,48,64]{0,2,1:T(8,128)(2,1)S(1)}, bf16[128,48,64]{0,2,1:T(8,128)(2,1)}, u32[]{:S(2)}) copy-start(bf16[128,48,64]{0,2,1:T(8,128)(2,1)} %get-tuple-element.310) | copy-start | bytes 2359300
  232.8 8.8 %copy-start.2 = (bf16[128,128,64]{1,2,0:T(8,128)(2,1)S(1)}, bf16[128,128,64]{1,2,0:T(8,128)(2,1)}, u32[]{:S(2)}) copy-start(bf16[128,128,64]{1,2,0:T(8,128)(2,1)} %gather_fusion.2) | copy-start | bytes 6291460
  232.8 25.5 %collective-permute-start.17 = (bf16[8,8192]{1,0:T(8,128)(2,1)S(1)}, bf16[8,8192]{1,0:T(8,128)(2,1)S(1)}, u32[]{:S(2)}, u32[]{:S(2)}) collective-permute-start(bf16[8,8192]{1,0:T(8,128)(2,1)S(1)} %fusion), channel_id=1, source_target_pairs={{0,3},{1,4},{2,5},{3,6},{4,7},{5,8},{6,9},{7,10},{8,11},{9,12},{10... | collective-permute-start | bytes 393224
  234.3 24.1 %collective-permute-start.16 = (bf16[8,8192]{1,0:T(8,128)(2,1)S(1)}, bf16[8,8192]{1,0:T(8,128)(2,1)S(1)}, u32[]{:S(2)}, u32[]{:S(2)}) collective-permute-start(bf16[8,8192]{1,0:T(8,128)(2,1)S(1)} %fusion), channel_id=1, source_target_pairs={{0,2},{1,3},{2,4},{3,5},{4,6},{5,7},{6,8},{7,9},{8,10},{9,11},{10,... | collective-permute-start | bytes 393224
  236.9 21.5 %collective-permute-start.15 = (bf16[8,8192]{1,0:T(8,128)(2,1)S(1)}, bf16[8,8192]{1,0:T(8,128)(2,1)S(1)}, u32[]{:S(2)}, u32[]{:S(2)}) collective-permute-start(bf16[8,8192]{1,0:T(8,128)(2,1)S(1)} %fusion), channel_id=1, source_target_pairs={{0,1},{1,2},{2,3},{3,4},{4,5},{5,6},{6,7},{7,8},{8,9},{9,10},{10,1... | collective-permute-start | bytes 393224
  245.7 10.1 %copy-start.4 = (pred[128]{0:T(512)(128)(4,1)S(1)}, pred[128]{0:T(512)(128)(4,1)}, u32[]{:S(2)}) copy-start(pred[128]{0:T(512)(128)(4,1)} %iota_compare_fusion) | copy-start | bytes 388
  249.1 9.3 %collective-permute-start.18 = (bf16[6,8192]{1,0:T(8,128)(2,1)S(1)}, bf16[6,8192]{1,0:T(8,128)(2,1)S(1)}, u32[]{:S(2)}, u32[]{:S(2)}) collective-permute-start(bf16[6,8192]{1,0:T(8,128)(2,1)S(1)} %slice.8), channel_id=1, source_target_pairs={{0,4},{1,5},{2,6},{3,7},{4,8},{5,9},{6,10},{7,11},{8,12},{9,13},{1... | collective-permute-start | bytes 294920
  (4 other events, 27.7 us)
Sparse Core Ops, SparseCore 0:
  23.7 56.8 all-gather.1
  258.5 147.3 all-reduce.7
